TPU v7x, 256 devices: a whole 4x4x8 slice. The times are simulated.
256 devices in a mesh: section: 16 (over z, x_lo), expert: 16 (over y, x_hi, core).
Axes of the slice: x: 4 (x_hi: 2, x_lo: 2; x = x_hi * 2 + x_lo), y: 4, z: 8, core: 2. Of those that a mesh axis runs over, the one named last changes fastest.
Arguments:
- state: bfloat16 [16, 2048, 4096], P('section', 'expert'), may hold values from -6 to 6
- lengths: int32 [16], P('section'), may hold values from 128 to 2048, as said below
- gain: float32 [16, 4096], P('section'), may hold values from 0.25 to 1.75
- w_gate: bfloat16 [16, 4096, 6144], P('section', None, 'expert'), may hold values from -0.09375 to 0.09375
- w_up: bfloat16 [16, 4096, 6144], P('section', None, 'expert'), may hold values from -0.09375 to 0.09375
- w_down: bfloat16 [16, 6144, 4096], P('section', 'expert'), may hold values from -0.21875 to 0.21875
- expert_ids: int32 [2, 16, 2048, 2], P(None, 'section', 'expert'), may hold values from 0 to 7, all different within a row; in each aligned block of 128 rows (0 to 127, 128 to 255, ..., all dimensions but the last counted through in order) at most 40 rows name the same one
- gate_weights: float32 [2, 16, 2048, 2], P(None, 'section', 'expert'), may hold values from 0.1 to 1
Outputs:
- hidden_out: bfloat16 [16, 2048, 4096], P('section', 'expert')
Inputs may be any that keep to these rules, and one draw needn't show every extreme that they name: `expert_ids`: in each aligned block of 128 rows (the rows of one device) no expert is named by more than 40 rows, a bound that some block reaches; a row names 2 different experts. `lengths`: live rows are a prefix of each micro-batch; the micro-batch at section 0 is full.
All inputs are finite; a program needn't handle non-finite values.
Results may differ from a plain program's by a relative error of at most 0.0059.
Values may be sent and summed in bfloat16 or wider, within the bound.
A program may use at most 128 MiB of HBM per device.

v0:
```python
import jax
import jax.numpy as jnp
from jax import lax
from jax.sharding import PartitionSpec as P

STEPS = 2


def shifted(array, axis, by):
    peers = lax.axis_size(axis)
    return lax.ppermute(array, axis, [(i, (i + by) % peers) for i in range(peers)])


def body(state, lengths, gain, w_gate, w_up, w_down, expert_ids, gate_weights):
    groups = lax.axis_size("expert")
    experts = groups // 2
    tok_rows = state.shape[1]
    width = state.shape[2]
    top = expert_ids.shape[3]
    capacity = min(tok_rows, 2 * (tok_rows * top * 5 // (8 * experts)))
    slots = experts * capacity
    row_index = lax.axis_index("expert") * tok_rows + jnp.arange(tok_rows, dtype=jnp.int32)
    gate_cols = w_gate[0]
    up_cols = w_up[0]
    down_rows = w_down[0]
    for step in range(STEPS):
        current = state[0]
        xf = current.astype(jnp.float32)
        normed = (
            xf * lax.rsqrt(jnp.mean(xf * xf, axis=-1, keepdims=True) + 1e-06) * gain[0]
        ).astype(jnp.bfloat16)
        valid = row_index < lengths[0]
        ids = expert_ids[step, 0]
        onehot = (
            (ids[:, :, None] == jnp.arange(experts, dtype=jnp.int32)) & valid[:, None, None]
        ).astype(jnp.int32)
        flat = onehot.reshape(tok_rows * top, experts)
        before = jnp.cumsum(flat, axis=0) - flat
        position = jnp.sum(before * flat, axis=-1).reshape(tok_rows, top)
        slot_of = jnp.where(valid[:, None], ids * capacity + position, -1)
        picks = (slot_of[:, :, None] == jnp.arange(slots, dtype=jnp.int32)).astype(jnp.bfloat16)
        chosen = jnp.sum(picks, axis=1)
        packed = jnp.dot(chosen.T, normed, preferred_element_type=jnp.float32).astype(jnp.bfloat16)
        packed = packed.reshape(experts, capacity, width)
        outgoing = jnp.repeat(packed, 2, axis=0)
        received = lax.all_to_all(outgoing, "expert", split_axis=0, concat_axis=0, tiled=True)
        count = received.shape[0] * received.shape[1]
        rows = received.reshape(count, width)
        gated = jnp.dot(rows, gate_cols, preferred_element_type=jnp.float32)
        upper = jnp.dot(rows, up_cols, preferred_element_type=jnp.float32)
        hidden = (jax.nn.silu(gated) * upper).astype(jnp.bfloat16)
        part = jnp.dot(hidden, down_rows, preferred_element_type=jnp.float32).astype(jnp.bfloat16)
        returned = lax.all_to_all(
            part.reshape(received.shape), "expert", split_axis=0, concat_axis=0, tiled=True
        )
        results = (
            returned.reshape(experts, 2, capacity, width)
            .astype(jnp.float32)
            .sum(axis=1)
            .astype(jnp.bfloat16)
        )
        results = results.reshape(slots, width)
        total = xf
        for pick in range(top):
            fetched = jnp.dot(picks[:, pick, :], results, preferred_element_type=jnp.float32)
            total = total + gate_weights[step, 0][:, pick : pick + 1] * fetched
        updated = total.astype(jnp.bfloat16)[None]
        state, lengths = shifted((updated, lengths), "section", 1)
    return state


def solution(mesh):
    return jax.shard_map(
        body,
        mesh=mesh,
        in_specs=(
            P("section", "expert", None),
            P("section"),
            P("section", None),
            P("section", None, "expert"),
            P("section", None, "expert"),
            P("section", "expert", None),
            P(None, "section", "expert", None),
            P(None, "section", "expert", None),
        ),
        out_specs=P("section", "expert", None),
        check_vma=False,
    )
```

profile of v0, /device:TPU:1, one launch (start us, length us, event | category | flops | bytes accessed | tf_op | source)
XLA Modules:
  0.0 393.5 jit_solution(8730237347020630341)
XLA Ops:
  0.0 0.8 fusion.68
  0.8 0.1 copy.19
  1.0 0.1 eq.82
  1.1 0.1 eq.78
  1.9 0.1 broadcast_in_dim.51
  2.0 0.1 broadcast_in_dim.52
  2.2 0.6 reduce-window.14
  2.8 0.2 slice_reduce_fusion.1
  3.0 0.1 broadcast_in_dim.50
  3.1 0.1 and.35
  3.3 0.1 fusion.55
  3.4 0.1 reshape.187
  3.5 0.1 fusion.51
  3.6 0.1 copy.16
  3.7 0.1 convert_reduce_fusion.1
  3.7 1.5 fusion.18
  5.3 2.2 convolution_convert_fusion.3
  7.4 0.6 broadcast_in_dim.54
  8.1 0.0 copy-start.6
  8.1 70.4 %all_to_all.20 = bf16[16,40,4096]{2,1,0:T(8,128)(2,1)S(1)} all-to-all(bf16[16,40,4096]{2,1,0:T(8,128)(2,1)S(1)} %bitcast.136), channel_id=1, replica_groups=mesh['section'=16,'expert'=16] {'expert'}, dimensions={0} | all-to-all | bytes 10485760 | tf_op jit(solution)/shard_map/all_to_all | solution.py:46
  78.5 2.3 copy-done.2
  80.8 3.8 fusion.16
  84.6 11.5 %convolution_convert_fusion.1 = bf16[640,4096]{1,0:T(8,128)(2,1)} fusion(bf16[1,384,4096]{2,1,0:T(8,128)(2,1)S(1)} %copy-done, bf16[640,4096]{1,0:T(8,128)(2,1)} %bitcast.143, bf16[1,4096,384]{2,1,0:T(8,128)(2,1)} %param.12, f32[640,384]{1,0:T(8,128)} %fusion.16), kind=kOutput, calls=%fused_computation.1 | convolution fusion | flops 4030627840 | bytes 17760256 | tf_op jit(solution)/shard_map/dot_general | solution.py:52
  96.2 5.6 %all-to-all-start.1 = ((bf16[16,40,4096]{2,1,0:T(8,128)(2,1)}), bf16[16,40,4096]{2,1,0:T(8,128)(2,1)}, u32[]{:S(2)}, u32[]{:S(2)}) async-start(bf16[16,40,4096]{2,1,0:T(8,128)(2,1)} %bitcast.140), calls=%async_computation.1 | async-start | bytes 10485760 | tf_op jit(solution)/shard_map/all_to_all | solution.py:53
  101.8 0.1 iota_compare_fusion.1
  101.9 62.3 %all-to-all-done.1 = bf16[16,40,4096]{2,1,0:T(8,128)(2,1)} async-done(((bf16[16,40,4096]{2,1,0:T(8,128)(2,1)}), bf16[16,40,4096]{2,1,0:T(8,128)(2,1)}, u32[]{:S(2)}, u32[]{:S(2)}) %all-to-all-start.1) | async-done | bytes 5242912 | tf_op jit(solution)/shard_map/all_to_all | solution.py:53
  164.2 4.0 %bitcast_reduce_fusion.1 = bf16[8,40,4096]{2,1,0:T(8,128)(2,1)S(1)} fusion(bf16[16,40,4096]{2,1,0:T(8,128)(2,1)} %all-to-all-done.1), kind=kLoop, calls=%fused_computation.5 | loop fusion | flops 1310720 | bytes 7864320 | tf_op jit(solution)/shard_map/reduce_sum | solution.py:59
  168.2 0.8 fusion.3
  169.0 1.7 fusion.7
  170.8 0.3 collective-permute-start
  171.1 2.5 collective-permute-start.1
  173.6 0.1 copy.20
  173.7 0.1 eq.93
  173.8 0.1 eq.89
  174.0 25.3 %collective-permute-done.1 = s32[1]{0:T(128)} collective-permute-done((s32[1]{0:T(128)}, s32[1]{0:T(128)}, u32[]{:S(2)}, u32[]{:S(2)}) %collective-permute-start.1) | collective-permute-done | bytes 36 | tf_op jit(solution)/shard_map/ppermute | solution.py:11
  199.3 0.7 fusion.62
  200.0 0.1 broadcast_in_dim.57
  200.1 0.1 broadcast_in_dim.58
  200.3 0.6 reduce-window.16
  200.8 0.2 slice_reduce_fusion
  201.1 0.7 fusion.64
  201.8 0.1 broadcast_in_dim.56
  201.9 0.1 and.40
  202.0 0.1 fusion.53
  202.1 0.1 reshape.195
  202.3 0.1 fusion.50
  202.4 0.1 copy.18
  202.4 0.1 convert_reduce_fusion
  202.5 1.5 fusion.21
  204.1 2.2 convolution_convert_fusion.2
  206.2 0.6 broadcast_in_dim.59
  206.9 67.3 %all_to_all.21 = bf16[16,40,4096]{2,1,0:T(8,128)(2,1)S(1)} all-to-all(bf16[16,40,4096]{2,1,0:T(8,128)(2,1)S(1)} %bitcast.137), channel_id=1, replica_groups=mesh['section'=16,'expert'=16] {'expert'}, dimensions={0} | all-to-all | bytes 10485760 | tf_op jit(solution)/shard_map/all_to_all | solution.py:46
  274.2 2.3 copy-done.3
  276.5 3.8 fusion.14
  280.3 11.5 %convolution_convert_fusion = bf16[640,4096]{1,0:T(8,128)(2,1)} fusion(bf16[1,384,4096]{2,1,0:T(8,128)(2,1)S(1)} %copy-done, bf16[640,4096]{1,0:T(8,128)(2,1)} %bitcast.145, bf16[1,4096,384]{2,1,0:T(8,128)(2,1)} %param.12, f32[640,384]{1,0:T(8,128)} %fusion.14), kind=kOutput, calls=%fused_computation | convolution fusion | flops 4030627840 | bytes 17760256 | tf_op jit(solution)/shard_map/dot_general | solution.py:52
  291.9 5.5 %all-to-all-start.3 = ((bf16[16,40,4096]{2,1,0:T(8,128)(2,1)}), bf16[16,40,4096]{2,1,0:T(8,128)(2,1)}, u32[]{:S(2)}, u32[]{:S(2)}) async-start(bf16[16,40,4096]{2,1,0:T(8,128)(2,1)} %bitcast.141), calls=%async_computation.3 | async-start | bytes 10485760 | tf_op jit(solution)/shard_map/all_to_all | solution.py:53
  297.4 0.1 iota_compare_fusion
  297.4 62.3 %all-to-all-done.3 = bf16[16,40,4096]{2,1,0:T(8,128)(2,1)} async-done(((bf16[16,40,4096]{2,1,0:T(8,128)(2,1)}), bf16[16,40,4096]{2,1,0:T(8,128)(2,1)}, u32[]{:S(2)}, u32[]{:S(2)}) %all-to-all-start.3) | async-done | bytes 5242912 | tf_op jit(solution)/shard_map/all_to_all | solution.py:53
  359.8 3.9 bitcast_reduce_fusion
  363.7 0.8 convolution_multiply_fusion
  364.5 2.1 fusion.6
  366.6 0.1 collective-permute-start.2
  366.7 25.8 %collective-permute-done.2 = bf16[1,128,4096]{2,1,0:T(8,128)(2,1)S(1)} collective-permute-done((bf16[1,128,4096]{2,1,0:T(8,128)(2,1)S(1)}, bf16[1,128,4096]{2,1,0:T(8,128)(2,1)S(1)}, u32[]{:S(2)}, u32[]{:S(2)}) %collective-permute-start.2) | collective-permute-done | bytes 1048608 | tf_op jit(solution)/shard_map/ppermute | solution.py:11
  392.5 1.0 copy.25
  (27 shorter events, 0.2 us)
Async XLA Ops:
  0.0 84.6 %copy-start = (bf16[1,384,4096]{2,1,0:T(8,128)(2,1)S(1)}, bf16[1,384,4096]{2,1,0:T(8,128)(2,1)}, u32[]{:S(2)}) copy-start(bf16[1,384,4096]{2,1,0:T(8,128)(2,1)} %param.13) | copy-start | bytes 9437188
  8.1 72.7 %copy-start.6 = (bf16[1,4096,384]{2,1,0:T(8,128)(2,1)S(1)}, bf16[1,4096,384]{2,1,0:T(8,128)(2,1)}, u32[]{:S(2)}) copy-start(bf16[1,4096,384]{2,1,0:T(8,128)(2,1)} %param.11) | copy-start | bytes 9437188
  78.5 2.3 copy-start.2
  96.2 5.6 %copy-start.5 = (f32[2,1,128,2]{2,3,1,0:T(2,128)S(1)}, f32[2,1,128,2]{2,3,1,0:T(2,128)}, u32[]{:S(2)}) copy-start(f32[2,1,128,2]{2,3,1,0:T(2,128)} %param.15) | copy-start | bytes 6148
  96.2 68.0 %all-to-all-start.1 = ((bf16[16,40,4096]{2,1,0:T(8,128)(2,1)}), bf16[16,40,4096]{2,1,0:T(8,128)(2,1)}, u32[]{:S(2)}, u32[]{:S(2)}) async-start(bf16[16,40,4096]{2,1,0:T(8,128)(2,1)} %bitcast.140), calls=%async_computation.1 | async-start | bytes 10485760 | tf_op jit(solution)/shard_map/all_to_all | solution.py:53
  164.2 4.0 %copy-start.1 = (bf16[1,128,4096]{2,1,0:T(8,128)(2,1)S(1)}, bf16[1,128,4096]{2,1,0:T(8,128)(2,1)}, u32[]{:S(2)}) copy-start(bf16[1,128,4096]{2,1,0:T(8,128)(2,1)} %param.8) | copy-start | bytes 3145732
  169.0 35.0 %copy-start.4 = (f32[1,4096]{1,0:T(1,128)S(1)}, f32[1,4096]{1,0:T(1,128)}, u32[]{:S(2)}) copy-start(f32[1,4096]{1,0:T(1,128)} %param.10) | copy-start | bytes 49156
  170.8 31.7 %collective-permute-start = (bf16[1,128,4096]{2,1,0:T(8,128)(2,1)}, bf16[1,128,4096]{2,1,0:T(8,128)(2,1)}, u32[]{:S(2)}, u32[]{:S(2)}) collective-permute-start(bf16[1,128,4096]{2,1,0:T(8,128)(2,1)} %fusion.7), channel_id=1, source_target_pairs={{0,16},{16,32},{32,48},{48,64},{64,80},{80,96},{96,112},{112,128},... | collective-permute-start | bytes 3145736 | tf_op jit(solution)/shard_map/ppermute | solution.py:11
  171.1 28.2 %collective-permute-start.1 = (s32[1]{0:T(128)}, s32[1]{0:T(128)}, u32[]{:S(2)}, u32[]{:S(2)}) collective-permute-start(s32[1]{0:T(128)} %param.9), channel_id=1, source_target_pairs={{0,16},{16,32},{32,48},{48,64},{64,80},{80,96},{96,112},{112,128},... | collective-permute-start | bytes 20 | tf_op jit(solution)/shard_map/ppermute | solution.py:11
  206.9 69.6 %copy-start.7 = (bf16[1,4096,384]{2,1,0:T(8,128)(2,1)S(1)}, bf16[1,4096,384]{2,1,0:T(8,128)(2,1)}, u32[]{:S(2)}) copy-start(bf16[1,4096,384]{2,1,0:T(8,128)(2,1)} %param.11) | copy-start | bytes 9437188
  274.2 2.3 copy-start.3
  291.9 67.9 %all-to-all-start.3 = ((bf16[16,40,4096]{2,1,0:T(8,128)(2,1)}), bf16[16,40,4096]{2,1,0:T(8,128)(2,1)}, u32[]{:S(2)}, u32[]{:S(2)}) async-start(bf16[16,40,4096]{2,1,0:T(8,128)(2,1)} %bitcast.141), calls=%async_computation.3 | async-start | bytes 10485760 | tf_op jit(solution)/shard_map/all_to_all | solution.py:53
  366.6 25.9 %collective-permute-start.2 = (bf16[1,128,4096]{2,1,0:T(8,128)(2,1)S(1)}, bf16[1,128,4096]{2,1,0:T(8,128)(2,1)S(1)}, u32[]{:S(2)}, u32[]{:S(2)}) collective-permute-start(bf16[1,128,4096]{2,1,0:T(8,128)(2,1)S(1)} %fusion.6), channel_id=1, source_target_pairs={{0,16},{16,32},{32,48},{48,64},{64,80},{80,96},{96,112},{112,128},... | collective-permute-start | bytes 3145736 | tf_op jit(solution)/shard_map/ppermute | solution.py:11
where the time goes:
time: 394 us; the launch traced here: 393 us
  waiting for transfers between devices  176 us (45%)
  blocking collectives  138 us (35%)
  matrix products  40.4 us (10%)
  other arithmetic  14.2 us (4%)
  starting transfers between devices  14 us (4%)
  local copies, waits for them, and re-layouts  10.4 us (3%)
    all_to_all x2, blocking collectives, body(): lax.all_to_all(outgoing, 'expert', split_axis=0, concat_axis=0, tiled=True)  138 us
    all_to_all x2, waiting for transfers between devices, body(): lax.all_to_all(part.reshape(received.shape), 'expert', split_axis=0, conc...  125 us
    ppermute x3, waiting for transfers between devices, shifted(): lax.ppermute(array, axis, [(i, (i + by) % peers) for i in range(peers)])  51.2 us
    dot_general x2, matrix products, body(): jnp.dot(hidden, down_rows, preferred_element_type=jnp.float32)  23.1 us
    all_to_all x2, starting transfers between devices, body(): lax.all_to_all(part.reshape(received.shape), 'expert', split_axis=0, conc...  11.1 us
    reduce_sum x2, other arithmetic, body(): results = returned.reshape(experts, 2, capacity, width).astype(jnp.float3...  7.92 us
  transfers between devices with their start and end apart: 5, of which 4 were waited for; matrix products, arithmetic and copies ran while one was open for 1% of the time, Pallas kernels for 0%

commit v1 on v0

v1 whole, which is shorter than its diff:
```python
import functools

import jax
import jax.numpy as jnp
from jax import lax
from jax.experimental import pallas as pl
from jax.experimental.pallas import tpu as pltpu
from jax.sharding import PartitionSpec as P

CAP = 40
CHIPS = 8
OWN = 2
CHUNKS = 4
GROUPS = 4
MESH = pl.DeviceIdType.MESH
F32 = jnp.float32
BF16 = jnp.bfloat16


def order(k):
    m = k % 4
    return (2 * m + 1 - m // 2) % 4, (k % 2 + k // 4) % 2


def kernel(
    x_ref, meta_ref, gain_ref, wg_ref, wu_ref, wd_ref, o_ref,
    xin, xb, ssb, meta0, meta1, metaz, gain1, wgu, wdn, normed, pick, pickw, pickt,
    packed, arrived, hidden, outgo, back, stage,
    w_sem, wd_send, wd_recv, x_send, x_recv, ss_send, ss_recv, m_send, m_recv,
    d_send, d_recv, f_send, f_recv, h_send, h_recv, c_send, c_recv, r_send, r_recv, o_send, o_recv, l_sem,
):
    rows = x_ref.shape[0]
    width = x_ref.shape[1]
    half = width // 2
    hid = wg_ref.shape[1]
    block = 2 * CAP
    cw = half // CHUNKS
    per = CHIPS // GROUPS
    section = lax.axis_index("section")
    expert = lax.axis_index("expert")
    depth = lax.axis_size("section") // 2
    z = section // 2
    x_lo = section % 2
    y = expert // 4
    x_hi = (expert // 2) % 2
    core = expert % 2
    other = 1 - core
    chip = expert // 2

    def device(dz=0, flip=0, dy=0, fxh=0, to=None):
        to = core if to is None else to
        return (
            ((z + dz + depth) % depth) * 2 + (x_lo + flip) % 2,
            (((y + dy + 4) % 4) * 2 + (x_hi + fxh) % 2) * 2 + to,
        )

    partner = device(to=other)
    mine = pl.multiple_of(core * half, half)
    theirs = pl.multiple_of(other * half, half)

    def remote(src, dst, send, recv, to):
        return pltpu.make_async_remote_copy(
            src_ref=src, dst_ref=dst, send_sem=send, recv_sem=recv, device_id=to, device_id_type=MESH
        )

    def loop(count, step):
        lax.fori_loop(0, count, lambda i, c: (step(i), c)[1], 0)

    hid_at = pl.multiple_of(core * hid, hid)
    weight_copies = [
        pltpu.make_async_copy(wg_ref, wgu.at[:, pl.ds(0, hid)], w_sem.at[0]),
        pltpu.make_async_copy(wu_ref, wgu.at[:, pl.ds(hid, hid)], w_sem.at[1]),
        pltpu.make_async_copy(wd_ref.at[:, pl.ds(mine, half)], wdn.at[pl.ds(hid_at, hid), :], w_sem.at[2]),
    ]
    own_x = pltpu.make_async_copy(x_ref.at[:, pl.ds(mine, half)], xb.at[0, core], l_sem.at[0])
    whole_x = pltpu.make_async_copy(x_ref, xin, l_sem.at[1])
    own_meta = pltpu.make_async_copy(meta_ref, meta0.at[core], l_sem.at[2])
    whole_x.start()
    own_x.start()
    own_meta.start()

    barrier = pltpu.get_barrier_semaphore()

    def greet(to):
        pl.semaphore_signal(barrier, inc=1, device_id=to, device_id_type=MESH)

    greet(partner)

    def greet_chips(k):
        dy, fxh = order(k)
        greet(device(flip=1, dy=dy, fxh=fxh))

        @pl.when(k != OWN)
        def _():
            greet(device(dy=dy, fxh=fxh))

    loop(CHIPS, greet_chips)
    greet(device(flip=1, to=other))
    for dz in (1, -1):
        for to in (core, other):
            greet(device(dz=dz, to=to))
    pl.semaphore_wait(barrier, 2 * CHIPS + 5)

    x_copy = remote(x_ref.at[:, pl.ds(theirs, half)], xb.at[0, core], x_send, x_recv, partner)
    meta_copies = [
        remote(meta_ref, meta0.at[core], m_send.at[0], m_recv.at[0], partner),
        remote(meta_ref, metaz, m_send.at[1], m_recv.at[1], device(dz=1)),
        remote(gain_ref, gain1, m_send.at[2], m_recv.at[2], device(flip=1)),
        remote(meta_ref, meta1.at[core], m_send.at[3], m_recv.at[3 + core], device(flip=1, to=core)),
        remote(meta_ref, meta1.at[core], m_send.at[4], m_recv.at[3 + core], device(flip=1, to=other)),
    ]
    meta_copies[0].start()
    x_copy.start()
    for copy in weight_copies:
        copy.start()
    whole_x.wait()
    xf = xin[...].astype(F32)
    ssb[0, core] = jnp.broadcast_to(jnp.sum(xf * xf, axis=-1, keepdims=True), (rows, 128))
    ss_copy = remote(ssb.at[0, core], ssb.at[0, core], ss_send.at[0], ss_recv.at[0], partner)
    ss_copy.start()
    for copy in meta_copies[1:]:
        copy.start()
    wd_copy = remote(
        wd_ref.at[:, pl.ds(theirs, half)], wdn.at[pl.ds(hid_at, hid), :], wd_send, wd_recv, partner
    )
    wd_copy.start()
    own_meta.wait()
    own_x.wait()
    meta_copies[0].wait()
    x_copy.wait()
    ss_copy.wait()

    sub8 = lax.broadcasted_iota(jnp.int32, (8, rows), 0).astype(F32)
    before = (
        lax.broadcasted_iota(jnp.int32, (rows, rows), 0) < lax.broadcasted_iota(jnp.int32, (rows, rows), 1)
    ).astype(BF16)
    lane = lax.broadcasted_iota(jnp.int32, (1, rows), 1)
    slot_no = lax.broadcasted_iota(jnp.int32, (block, rows), 0).astype(F32)

    for step in range(2):
        flip = step
        meta = meta1 if step else meta0

        choices = []
        for part in range(2):
            if step == 0:
                length = meta0[part, 8:9, :]
            else:
                length = jnp.where(x_lo == 0, meta0[0, 8:9, :], metaz[8:9, :])
            live = ((chip * 2 + part) * rows + lane).astype(F32) < length
            ids = [meta[part, 2 * step + k : 2 * step + k + 1, :] for k in range(2)]
            gates = [meta[part, 4 + 2 * step + k : 5 + 2 * step + k, :] for k in range(2)]
            ones = [jnp.where((i == sub8) & live, 1.0, 0.0) for i in ids]
            earlier = jnp.dot((ones[0] + ones[1]).astype(BF16), before, preferred_element_type=F32)
            slots = [
                jnp.where(live, jnp.sum(earlier * one, axis=0, keepdims=True) + float(part * CAP), -1.0)
                for one in ones
            ]
            choices.append((ids, gates, slots))

        gain = gain1 if step else gain_ref
        for part in range(2):
            if step == 0:
                total = ssb[0, part, :, 0:1]
            else:
                total = ssb[1, part, :, 0:1] + ssb[2, part, :, 0:1]
            scale = lax.rsqrt(total * (1.0 / width) + 1e-06)
            normed[part * rows : (part + 1) * rows, :] = (
                xb[step, part].astype(F32) * scale * gain[0:1, pl.ds(mine, half)]
            ).astype(BF16)

        def dispatch(k):
            dy, fxh = order(k)
            return remote(
                packed.at[k], arrived.at[step, core, k], d_send.at[k], d_recv.at[step, k],
                device(flip=flip, dy=dy, fxh=fxh),
            )

        def pack(k):
            dy, fxh = order(k)
            target = (((y + dy) % 4) * 2 + (x_hi + fxh) % 2).astype(F32)
            hits, weighted = [], []
            for ids, gates, slots in choices:
                match = [jnp.where((ids[i] == target) & (slots[i] == slot_no), 1.0, 0.0) for i in range(2)]
                hits.append(match[0] + match[1])
                weighted.append(match[0] * gates[0] + match[1] * gates[1])
            pick[...] = jnp.concatenate(hits, axis=1).astype(BF16)
            pickw[k] = jnp.concatenate(weighted, axis=1)
            sent = jnp.dot(pick[...], normed[...], preferred_element_type=F32).astype(BF16)
            if step == 0:

                @pl.when(k == OWN)
                def _():
                    arrived[0, core, OWN] = sent

                @pl.when(k != OWN)
                def _():
                    packed[k] = sent
                    dispatch(k).start()
            else:
                packed[k] = sent
                dispatch(k).start()

        loop(CHIPS, pack)

        turned = pickw[...].reshape(CHIPS * block, 2 * rows).T
        high = turned.astype(BF16)
        pickt[0] = high
        pickt[1] = (turned - high.astype(F32)).astype(BF16)

        if step == 0:
            for copy in weight_copies:
                copy.wait()

        def forward(k):
            return remote(
                arrived.at[step, core, k], arrived.at[step, core, k], f_send.at[k], f_recv.at[step, k], partner
            )

        def forwarded(k):
            return remote(
                arrived.at[step, other, k], arrived.at[step, other, k], f_send.at[k], f_recv.at[step, k], partner
            )

        def share(g):
            place = hidden.at[step, pl.ds(pl.multiple_of(g * per * block, per * block), per * block), pl.ds(hid_at, hid)]
            return remote(place, place, h_send.at[g], h_recv.at[step, g], partner)

        def serve(g):
            for i in range(per):
                k = g * per + i
                if step == 0:

                    @pl.when(k != OWN)
                    def _():
                        dispatch(k).wait_recv()
                else:
                    dispatch(k).wait_recv()
                forward(k).start()
            for i in range(per):
                forwarded(g * per + i).wait_recv()
            both = [
                arrived[step, side, pl.ds(g * per, per)].reshape(per * block, half) for side in range(2)
            ]
            product = jnp.dot(both[0], wgu[0:half, :], preferred_element_type=F32)
            product = product + jnp.dot(both[1], wgu[half:width, :], preferred_element_type=F32)
            value = (jax.nn.silu(product[:, 0:hid]) * product[:, hid:]).astype(BF16)
            hidden[step, pl.ds(pl.multiple_of(g * per * block, per * block), per * block), pl.ds(hid_at, hid)] = value
            share(g).start()

        loop(GROUPS, serve)

        if step == 0:
            wd_copy.wait()
        hid_there = pl.multiple_of(other * hid, hid)

        def shared(g):
            place = hidden.at[step, pl.ds(pl.multiple_of(g * per * block, per * block), per * block), pl.ds(hid_there, hid)]
            return remote(place, place, h_send.at[g], h_recv.at[step, g], partner)

        loop(GROUPS, lambda g: shared(g).wait_recv())

        def give(q, k):
            dy, fxh = order(k)
            return remote(
                outgo.at[q, k], back.at[step, q, k], c_send.at[q, k], c_recv.at[step, q, k],
                device(flip=flip, dy=-dy, fxh=fxh),
            )

        for q in range(CHUNKS):

            def finish(g):
                at = pl.multiple_of(g * per * block, per * block)
                value = jnp.dot(
                    hidden[step, pl.ds(at, per * block), :], wdn[:, q * cw : (q + 1) * cw],
                    preferred_element_type=F32,
                ).astype(BF16).reshape(per, block, cw)
                for i in range(per):
                    k = g * per + i
                    if step == 0:

                        @pl.when(k == OWN)
                        def _():
                            back[0, q, OWN] = value[i]

                        @pl.when(k != OWN)
                        def _():
                            outgo[q, k] = value[i]
                            give(q, k).start()
                    else:
                        outgo[q, k] = value[i]
                        give(q, k).start()

            loop(GROUPS, finish)

        def relay(q):
            return remote(
                stage.at[0, q], xb.at[1, :, :, pl.ds(q * cw, cw)], r_send.at[q], r_recv.at[q], device(dz=1)
            )

        def hand(q, part, dz):
            columns = pl.ds(pl.multiple_of(core * half + q * cw, cw), cw)
            return remote(
                stage.at[1, q, part], o_ref.at[:, columns], o_send.at[q, part], o_recv.at[q, core],
                device(dz=dz, to=part),
            )

        def keep(q):
            columns = pl.ds(pl.multiple_of(core * half + q * cw, cw), cw)
            return pltpu.make_async_copy(stage.at[1, q, core], o_ref.at[:, columns], l_sem.at[3 + q])

        for q in range(CHUNKS):

            def landed(k):
                if step == 0:

                    @pl.when(k != OWN)
                    def _():
                        give(q, k).wait_recv()
                else:
                    give(q, k).wait_recv()

            loop(CHIPS, landed)
            results = back[step, q].reshape(CHIPS * block, cw)
            for part in range(2):
                value = jnp.dot(pickt[0, part * rows : (part + 1) * rows, :], results, preferred_element_type=F32)
                value = value + jnp.dot(
                    pickt[1, part * rows : (part + 1) * rows, :], results, preferred_element_type=F32
                )
                value = (xb[step, part, :, q * cw : (q + 1) * cw].astype(F32) + value).astype(BF16)
                stage[step, q, part] = value

            if step == 0:

                @pl.when(x_lo == 1)
                def _():
                    relay(q).start()

                @pl.when(x_lo == 0)
                def _():
                    xb[1, :, :, q * cw : (q + 1) * cw] = stage[0, q]
            else:

                @pl.when(x_lo == 0)
                def _():
                    for part in range(2):
                        hand(q, part, 1).start()

                @pl.when(x_lo == 1)
                def _():
                    hand(q, other, 0).start()
                    keep(q).start()

        def sent_all(k):
            forward(k).wait_send()
            if step == 0:

                @pl.when(k != OWN)
                def _():
                    dispatch(k).wait_send()
                    for q in range(CHUNKS):
                        give(q, k).wait_send()
            else:
                dispatch(k).wait_send()
                for q in range(CHUNKS):
                    give(q, k).wait_send()

        if step == 0:
            for copy in meta_copies[1:3]:
                copy.wait()
            for copy in meta_copies[3:]:
                copy.wait_send()
            for part in range(2):
                remote(
                    meta_ref, meta1.at[part], m_send.at[3], m_recv.at[3 + part], device(flip=1, to=part)
                ).wait_recv()

            @pl.when(x_lo == 1)
            def _():
                for q in range(CHUNKS):
                    relay(q).wait()

            for part in range(2):
                value = xb[1, part].astype(F32)
                ssb[1, part] = jnp.broadcast_to(jnp.sum(value * value, axis=-1, keepdims=True), (rows, 128))
            sums = remote(ssb.at[1], ssb.at[2], ss_send.at[1], ss_recv.at[1], partner)
            sums.start()
            loop(CHIPS, sent_all)
            loop(GROUPS, lambda g: share(g).wait_send())
            sums.wait()
        else:
            loop(CHIPS, sent_all)
            loop(GROUPS, lambda g: share(g).wait_send())

            @pl.when(x_lo == 0)
            def _():
                for q in range(CHUNKS):
                    for part in range(2):
                        hand(q, part, 1).wait_send()

            @pl.when(x_lo == 1)
            def _():
                for q in range(CHUNKS):
                    hand(q, other, 0).wait_send()
                    keep(q).wait()

            def taken(q, part):
                columns = pl.ds(part * half + q * cw, cw)
                remote(
                    stage.at[1, q, 0], o_ref.at[:, columns], o_send.at[q, 0], o_recv.at[q, part], partner
                ).wait_recv()

            @pl.when(x_lo == 0)
            def _():
                for q in range(CHUNKS):
                    for part in range(2):
                        taken(q, part)

            @pl.when((x_lo == 1) & (core == 0))
            def _():
                for q in range(CHUNKS):
                    taken(q, 1)

            @pl.when((x_lo == 1) & (core == 1))
            def _():
                for q in range(CHUNKS):
                    taken(q, 0)


def body(state, lengths, gain, w_gate, w_up, w_down, expert_ids, gate_weights):
    rows, width = state.shape[1:]
    hid = w_gate.shape[2]
    half = width // 2
    block = 2 * CAP
    cw = half // CHUNKS
    meta = jnp.concatenate(
        [
            expert_ids[:, 0].transpose(0, 2, 1).reshape(4, rows).astype(F32),
            gate_weights[:, 0].transpose(0, 2, 1).reshape(4, rows),
            jnp.broadcast_to(lengths.astype(F32)[:, None], (8, rows)),
        ],
        axis=0,
    )
    vmem = pl.BlockSpec(memory_space=pltpu.VMEM)
    anywhere = pl.BlockSpec(memory_space=pl.ANY)
    dma = pltpu.SemaphoreType.DMA
    out = pl.pallas_call(
        kernel,
        out_shape=jax.ShapeDtypeStruct((rows, width), BF16),
        in_specs=[anywhere, vmem, vmem, anywhere, anywhere, anywhere],
        out_specs=anywhere,
        scratch_shapes=[
            pltpu.VMEM((rows, width), BF16),
            pltpu.VMEM((2, 2, rows, half), BF16),
            pltpu.VMEM((3, 2, rows, 128), F32),
            pltpu.VMEM((2, 16, rows), F32),
            pltpu.VMEM((2, 16, rows), F32),
            pltpu.VMEM((16, rows), F32),
            pltpu.VMEM((1, width), F32),
            pltpu.VMEM((width, 2 * hid), BF16),
            pltpu.VMEM((2 * hid, half), BF16),
            pltpu.VMEM((2 * rows, half), BF16),
            pltpu.VMEM((block, 2 * rows), BF16),
            pltpu.VMEM((CHIPS, block, 2 * rows), F32),
            pltpu.VMEM((2, 2 * rows, CHIPS * block), BF16),
            pltpu.VMEM((CHIPS, block, half), BF16),
            pltpu.VMEM((2, 2, CHIPS, block, half), BF16),
            pltpu.VMEM((2, CHIPS * block, 2 * hid), BF16),
            pltpu.VMEM((CHUNKS, CHIPS, block, cw), BF16),
            pltpu.VMEM((2, CHUNKS, CHIPS, block, cw), BF16),
            pltpu.VMEM((2, CHUNKS, 2, rows, cw), BF16),
            dma((3,)),
            dma, dma,
            dma, dma,
            dma((2,)), dma((2,)),
            dma((5,)), dma((5,)),
            dma((CHIPS,)), dma((2, CHIPS)),
            dma((CHIPS,)), dma((2, CHIPS)),
            dma((GROUPS,)), dma((2, GROUPS)),
            dma((CHUNKS, CHIPS)), dma((2, CHUNKS, CHIPS)),
            dma((CHUNKS,)), dma((CHUNKS,)),
            dma((CHUNKS, 2)), dma((CHUNKS, 2)),
            dma((3 + CHUNKS,)),
        ],
        compiler_params=pltpu.CompilerParams(
            collective_id=0, has_side_effects=True, vmem_limit_bytes=58 * 2**20
        ),
        cost_estimate=pl.CostEstimate(
            flops=2 * 2 * CHIPS * block * width * 3 * hid, bytes_accessed=3 * width * hid * 2 + 2 * rows * width * 2,
            transcendentals=0,
        ),
    )(state[0], meta, gain, w_gate[0], w_up[0], w_down[0])
    return out[None]


def solution(mesh):
    return jax.shard_map(
        body,
        mesh=mesh,
        in_specs=(
            P("section", "expert", None),
            P("section"),
            P("section", None),
            P("section", None, "expert"),
            P("section", None, "expert"),
            P("section", "expert", None),
            P(None, "section", "expert", None),
            P(None, "section", "expert", None),
        ),
        out_specs=P("section", "expert", None),
        check_vma=False,
    )
```

time: 394 us -> 178 us (0.45)
  the two profiles are of different devices: /device:TPU:1 before, /device:TPU:57 now
where the time goes in v1:
time: 178 us
  Pallas kernels  173 us (97%)
  local copies, waits for them, and re-layouts  2.37 us (1%)
  other arithmetic  2.03 us (1%)
    pallas_call x1, Pallas kernels, body(): pl.pallas_call(kernel, out_shape=jax.ShapeDtypeStruct((rows, width), BF16...  173 us

profile of v1, /device:TPU:57, one launch (start us, length us, event | category | flops | bytes accessed | tf_op | source)
XLA Modules:
  0.0 178.0 jit_solution(16483210534712447260)
XLA Ops:
  0.7 0.1 pad.2.clone
  0.7 0.7 convert_element_type.15
  1.4 1.4 maximum_maximum_fusion.meta_ref
  2.8 172.9 %shard_map.82 = bf16[128,4096]{1,0:T(8,128)(2,1)} custom-call(bf16[128,4096]{1,0:T(8,128)(2,1)} %bitcast.22, f32[16,128]{1,0:T(8,128)} %maximum_maximum_fusion.meta_ref, f32[1,4096]{1,0:T(1,128)} %gain_ref.1, bf16[4096,384]{1,0:T(8,128)(2,1)} %bitcast.19, bf16[4096,384]{1,0:T(8,128)(2,1)} %bitcast.20, bf16[384,4096]{1,0:T(8,128)(2,1)} %bitcast.21), custom_call_target="tpu_custom_call" | custom-call | flops 12079595520 | bytes 11534336 | tf_op jit(solution)/shard_map/pallas_call | solution.py:447
  175.7 2.3 %copy.11 = bf16[1,128,4096]{2,1,0:T(8,128)(2,1)} copy(bf16[1,128,4096]{2,1,0:T(8,128)(2,1)} %bitcast.16) | data formatting | bytes 2097152
  (1 shorter events, 0.0 us)

commit v2 on v1

v2 whole, which is shorter than its diff:
```python
import functools

import jax
import jax.numpy as jnp
from jax import lax
from jax.experimental import pallas as pl
from jax.experimental.pallas import tpu as pltpu
from jax.sharding import PartitionSpec as P

CAP = 40
CHIPS = 8
OWN = 2
CHUNKS = 8
GROUPS = 4
EARLY = 2
MESH = pl.DeviceIdType.MESH
F32 = jnp.float32
BF16 = jnp.bfloat16


def order(k):
    m = k % 4
    return (2 * m + 1 - m // 2) % 4, (k % 2 + k // 4) % 2


def kernel(
    x_ref, meta_ref, gain_ref, wg_ref, wu_ref, wd_ref, o_ref,
    xin, xb, ssb, ssl, meta0, meta1, metaz, gain1, wgu, wdn, normed, pick, pickw, pickt,
    packed, arrived, hidden, outgo, back, stage,
    w_sem, wd_send, wd_recv, x_send, x_recv, ss_send, ss_recv, m_send, m_recv,
    d_send, d_recv, f_send, f_recv, h_send, h_recv, c_send, c_recv, r_send, r_recv, o_send, o_recv, l_sem,
):
    rows = x_ref.shape[0]
    width = x_ref.shape[1]
    half = width // 2
    hid = wg_ref.shape[1]
    block = 2 * CAP
    cw = half // CHUNKS
    per = CHIPS // GROUPS
    section = lax.axis_index("section")
    expert = lax.axis_index("expert")
    depth = lax.axis_size("section") // 2
    z = section // 2
    x_lo = section % 2
    y = expert // 4
    x_hi = (expert // 2) % 2
    core = expert % 2
    other = 1 - core
    chip = expert // 2

    def device(dz=0, flip=0, dy=0, fxh=0, to=None):
        to = core if to is None else to
        return (
            ((z + dz + depth) % depth) * 2 + (x_lo + flip) % 2,
            (((y + dy + 4) % 4) * 2 + (x_hi + fxh) % 2) * 2 + to,
        )

    partner = device(to=other)
    mine = pl.multiple_of(core * half, half)
    theirs = pl.multiple_of(other * half, half)

    def remote(src, dst, send, recv, to):
        return pltpu.make_async_remote_copy(
            src_ref=src, dst_ref=dst, send_sem=send, recv_sem=recv, device_id=to, device_id_type=MESH
        )

    def loop(first, last, step):
        lax.fori_loop(first, last, lambda i, c: (step(i), c)[1], 0)

    hid_at = pl.multiple_of(core * hid, hid)
    hid_there = pl.multiple_of(other * hid, hid)
    weight_copies = [
        pltpu.make_async_copy(wg_ref, wgu.at[:, pl.ds(0, hid)], w_sem.at[0]),
        pltpu.make_async_copy(wu_ref, wgu.at[:, pl.ds(hid, hid)], w_sem.at[1]),
        pltpu.make_async_copy(wd_ref.at[:, pl.ds(mine, half)], wdn.at[pl.ds(hid_at, hid), :], w_sem.at[2]),
    ]
    own_x = pltpu.make_async_copy(x_ref.at[:, pl.ds(mine, half)], xb.at[0, core], l_sem.at[0])
    whole_x = pltpu.make_async_copy(x_ref, xin, l_sem.at[1])
    own_meta = pltpu.make_async_copy(meta_ref, meta0.at[core], l_sem.at[2])
    whole_x.start()
    own_x.start()
    own_meta.start()

    barrier = pltpu.get_barrier_semaphore()

    def greet(to):
        pl.semaphore_signal(barrier, inc=1, device_id=to, device_id_type=MESH)

    greet(partner)

    def greet_chips(k):
        dy, fxh = order(k)
        greet(device(flip=1, dy=dy, fxh=fxh))

        @pl.when(k != OWN)
        def _():
            greet(device(dy=dy, fxh=fxh))

    loop(0, CHIPS, greet_chips)
    greet(device(flip=1, to=other))
    for dz in (1, -1):
        for to in (core, other):
            greet(device(dz=dz, to=to))
    for copy in weight_copies:
        copy.start()
    whole_x.wait()
    xf = xin[...].astype(F32)
    ssb[0, core] = jnp.broadcast_to(jnp.sum(xf * xf, axis=-1, keepdims=True), (rows, 128))
    pl.semaphore_wait(barrier, 2 * CHIPS + 5)

    x_copy = remote(x_ref.at[:, pl.ds(theirs, half)], xb.at[0, core], x_send, x_recv, partner)
    meta_copies = [
        remote(meta_ref, meta0.at[core], m_send.at[0], m_recv.at[0], partner),
        remote(meta_ref, metaz, m_send.at[1], m_recv.at[1], device(dz=1)),
        remote(gain_ref, gain1, m_send.at[2], m_recv.at[2], device(flip=1)),
        remote(meta_ref, meta1.at[core], m_send.at[3], m_recv.at[3 + core], device(flip=1, to=core)),
        remote(meta_ref, meta1.at[core], m_send.at[4], m_recv.at[3 + core], device(flip=1, to=other)),
    ]
    ss_copy = remote(ssb.at[0, core], ssb.at[0, core], ss_send.at[0], ss_recv.at[0], partner)
    meta_copies[0].start()
    x_copy.start()
    ss_copy.start()
    for copy in meta_copies[1:]:
        copy.start()
    wd_copy = remote(
        wd_ref.at[:, pl.ds(theirs, half)], wdn.at[pl.ds(hid_at, hid), :], wd_send, wd_recv, partner
    )
    wd_copy.start()

    sub8 = lax.broadcasted_iota(jnp.int32, (8, rows), 0).astype(F32)
    before = (
        lax.broadcasted_iota(jnp.int32, (rows, rows), 0) < lax.broadcasted_iota(jnp.int32, (rows, rows), 1)
    ).astype(BF16)
    lane = lax.broadcasted_iota(jnp.int32, (1, rows), 1)
    slot_no = lax.broadcasted_iota(jnp.int32, (block, rows), 0).astype(F32)

    def choose(step):
        meta = meta1 if step else meta0
        choices = []
        for part in range(2):
            if step == 0:
                length = meta0[part, 8:9, :]
            else:
                length = jnp.where(x_lo == 0, meta0[0, 8:9, :], metaz[8:9, :])
            live = ((chip * 2 + part) * rows + lane).astype(F32) < length
            ids = [meta[part, 2 * step + k : 2 * step + k + 1, :] for k in range(2)]
            gates = [meta[part, 4 + 2 * step + k : 5 + 2 * step + k, :] for k in range(2)]
            ones = [jnp.where((i == sub8) & live, 1.0, 0.0) for i in ids]
            earlier = jnp.dot((ones[0] + ones[1]).astype(BF16), before, preferred_element_type=F32)
            slots = [
                jnp.where(live, jnp.sum(earlier * one, axis=0, keepdims=True) + float(part * CAP), -1.0)
                for one in ones
            ]
            choices.append((ids, gates, slots))

        def match_chip(k):
            dy, fxh = order(k)
            target = (((y + dy) % 4) * 2 + (x_hi + fxh) % 2).astype(F32)
            hits, weighted = [], []
            for ids, gates, slots in choices:
                match = [jnp.where((ids[i] == target) & (slots[i] == slot_no), 1.0, 0.0) for i in range(2)]
                hits.append(match[0] + match[1])
                weighted.append(match[0] * gates[0] + match[1] * gates[1])
            pick[k] = jnp.concatenate(hits, axis=1).astype(BF16)
            pickw[k] = jnp.concatenate(weighted, axis=1)

        loop(0, CHIPS, match_chip)

    def turn(step):
        turned = pickw[...].reshape(CHIPS * block, 2 * rows).T
        high = turned.astype(BF16)
        pickt[step, 0 : 2 * rows] = high
        pickt[step, 2 * rows :] = (turned - high.astype(F32)).astype(BF16)

    def norm(step, part, total):
        gain = gain1 if step else gain_ref
        scale = lax.rsqrt(total * (1.0 / width) + 1e-06)
        normed[pl.ds(pl.multiple_of(part * rows, rows), rows), :] = (
            xb[step, part].astype(F32) * scale * gain[0:1, pl.ds(mine, half)]
        ).astype(BF16)

    own_meta.wait()
    meta_copies[0].wait()
    choose(0)

    for step in range(2):
        flip = step

        if step == 0:
            own_x.wait()
            norm(0, core, ssb[0, core, :, 0:1])
            x_copy.wait()
            ss_copy.wait()
            norm(0, other, ssb[0, other, :, 0:1])
        else:
            for part in range(2):
                norm(1, part, jnp.sum(ssb[1, part] + ssb[2, part], axis=-1, keepdims=True))

        def dispatch(k):
            dy, fxh = order(k)
            return remote(
                packed.at[k], arrived.at[step, core, k], d_send.at[k], d_recv.at[step, k],
                device(flip=flip, dy=dy, fxh=fxh),
            )

        for pair in range(CHIPS // 2):
            sent = jnp.dot(
                pick[2 * pair : 2 * pair + 2].reshape(2 * block, 2 * rows), normed[...], preferred_element_type=F32
            ).astype(BF16).reshape(2, block, half)
            for i in range(2):
                k = 2 * pair + i
                if step == 0 and k == OWN:
                    arrived[0, core, OWN] = sent[i]
                else:
                    packed[k] = sent[i]
                    dispatch(k).start()

        if step == 0:
            turn(0)
            for copy in weight_copies:
                copy.wait()
            wd_copy.wait()

        def forward(k, side):
            place = arrived.at[step, side, k]
            return remote(place, place, f_send.at[k], f_recv.at[step, k], partner)

        def share(g, at):
            place = hidden.at[
                step, pl.ds(pl.multiple_of(g * per * block, per * block), per * block), pl.ds(at, hid)
            ]
            return remote(place, place, h_send.at[g], h_recv.at[step, g], partner)

        def serve(g):
            for i in range(per):
                k = g * per + i
                if step == 0:

                    @pl.when(k != OWN)
                    def _():
                        dispatch(k).wait_recv()
                else:
                    dispatch(k).wait_recv()
                forward(k, core).start()
            for i in range(per):
                forward(g * per + i, other).wait_recv()
            both = [
                arrived[step, side, pl.ds(g * per, per)].reshape(per * block, half) for side in range(2)
            ]
            product = jnp.dot(both[0], wgu[0:half, :], preferred_element_type=F32)
            product = product + jnp.dot(both[1], wgu[half:width, :], preferred_element_type=F32)
            value = (jax.nn.silu(product[:, 0:hid]) * product[:, hid:]).astype(BF16)
            hidden[step, pl.ds(pl.multiple_of(g * per * block, per * block), per * block), pl.ds(hid_at, hid)] = value
            share(g, hid_at).start()

        def give(q, k):
            dy, fxh = order(k)
            return remote(
                outgo.at[q, k], back.at[step, q, k], c_send.at[q, k], c_recv.at[step, q, k],
                device(flip=flip, dy=-dy, fxh=fxh),
            )

        def finish(q, first, count):
            value = jnp.dot(
                hidden[step, first * per * block : (first + count) * per * block, :],
                wdn[:, pl.ds(pl.multiple_of(q * cw, cw), cw)],
                preferred_element_type=F32,
            ).astype(BF16).reshape(count * per, block, cw)
            for i in range(count * per):
                k = first * per + i
                if step == 0 and k == OWN:
                    back[0, q, OWN] = value[i]
                else:
                    outgo[q, k] = value[i]
                    give(q, k).start()

        loop(0, GROUPS - 1, serve)
        loop(0, GROUPS - 1, lambda g: share(g, hid_there).wait_recv())
        loop(0, EARLY, lambda q: finish(q, 0, GROUPS - 1))
        serve(GROUPS - 1)
        share(GROUPS - 1, hid_there).wait_recv()
        loop(0, EARLY, lambda q: finish(q, GROUPS - 1, 1))
        loop(EARLY, CHUNKS, lambda q: finish(q, 0, GROUPS))

        if step == 0:
            for copy in meta_copies[1:3]:
                copy.wait()
            for copy in meta_copies[3:]:
                copy.wait_send()
            for part in range(2):
                remote(
                    meta_ref, meta1.at[part], m_send.at[3], m_recv.at[3 + part], device(flip=1, to=part)
                ).wait_recv()
            choose(1)
            turn(1)

        def relay(q):
            return remote(
                stage.at[0, q], xb.at[1, :, :, pl.ds(pl.multiple_of(q * cw, cw), cw)],
                r_send.at[q], r_recv.at[q], device(dz=1),
            )

        def hand(q, part, dz):
            columns = pl.ds(pl.multiple_of(core * half + q * cw, cw), cw)
            return remote(
                stage.at[1, q, part], o_ref.at[:, columns], o_send.at[q, part], o_recv.at[q, core],
                device(dz=dz, to=part),
            )

        def keep(q):
            columns = pl.ds(pl.multiple_of(core * half + q * cw, cw), cw)
            return pltpu.make_async_copy(stage.at[1, q, core], o_ref.at[:, columns], l_sem.at[3 + q])

        def combine(q):
            for k in range(CHIPS):
                if not (step == 0 and k == OWN):
                    give(q, k).wait_recv()
            at = pl.multiple_of(q * cw, cw)
            value = jnp.dot(
                pickt[step], back[step, q].reshape(CHIPS * block, cw), preferred_element_type=F32
            )
            for part in range(2):
                low = (2 + part) * rows
                new = (
                    xb[step, part, :, pl.ds(at, cw)].astype(F32)
                    + (value[part * rows : (part + 1) * rows] + value[low : low + rows])
                ).astype(BF16)
                stage[step, q, part] = new
                if step == 0:
                    square = new.astype(F32) * new.astype(F32)
                    sums = square[:, 0:128]
                    for i in range(1, cw // 128):
                        sums = sums + square[:, i * 128 : (i + 1) * 128]
                    ssl[part] += sums

            if step == 0:

                @pl.when(x_lo == 1)
                def _():
                    relay(q).start()

                @pl.when(x_lo == 0)
                def _():
                    xb[1, :, :, pl.ds(at, cw)] = stage[0, q]
            else:

                @pl.when(x_lo == 0)
                def _():
                    for part in range(2):
                        hand(q, part, 1).start()

                @pl.when(x_lo == 1)
                def _():
                    hand(q, other, 0).start()
                    keep(q).start()

        if step == 0:
            ssl[...] = jnp.zeros_like(ssl)
        loop(0, CHUNKS, combine)

        def sent_all(k):
            forward(k, core).wait_send()
            if step == 0:

                @pl.when(k != OWN)
                def _():
                    dispatch(k).wait_send()
                    loop(0, CHUNKS, lambda q: give(q, k).wait_send())
            else:
                dispatch(k).wait_send()
                loop(0, CHUNKS, lambda q: give(q, k).wait_send())

        def all_sent():
            loop(0, CHIPS, sent_all)
            loop(0, GROUPS, lambda g: share(g, hid_at).wait_send())

        if step == 0:
            def sums(to, dz, number, sender):
                return remote(ssl, ssb.at[1 + sender], ss_send.at[number], ss_recv.at[1 + sender], device(dz=dz, to=to))

            @pl.when(x_lo == 0)
            def _():
                sums(other, 0, 1, core).start()
                ssb[1 + core] = ssl[...]
                all_sent()
                sums(other, 0, 1, core).wait_send()
                sums(other, 0, 1, other).wait_recv()

            @pl.when(x_lo == 1)
            def _():
                sums(core, 1, 1, core).start()
                sums(other, 1, 2, core).start()
                all_sent()
                loop(0, CHUNKS, lambda q: relay(q).wait())
                for number, sender in ((1, core), (2, other)):
                    sums(sender, 1, number, core).wait_send()
                    sums(sender, 1, number, sender).wait_recv()
        else:
            all_sent()

            @pl.when(x_lo == 0)
            def _():
                for part in range(2):
                    loop(0, CHUNKS, lambda q: hand(q, part, 1).wait_send())

            @pl.when(x_lo == 1)
            def _():
                loop(0, CHUNKS, lambda q: hand(q, other, 0).wait_send())
                loop(0, CHUNKS, lambda q: keep(q).wait())

            def taken(q, part):
                columns = pl.ds(pl.multiple_of(part * half + q * cw, cw), cw)
                remote(
                    stage.at[1, q, 0], o_ref.at[:, columns], o_send.at[q, 0], o_recv.at[q, part], partner
                ).wait_recv()

            @pl.when(x_lo == 0)
            def _():
                for part in range(2):
                    loop(0, CHUNKS, lambda q: taken(q, part))

            @pl.when(x_lo == 1)
            def _():
                loop(0, CHUNKS, lambda q: taken(q, other))


def body(state, lengths, gain, w_gate, w_up, w_down, expert_ids, gate_weights):
    rows, width = state.shape[1:]
    hid = w_gate.shape[2]
    half = width // 2
    block = 2 * CAP
    cw = half // CHUNKS
    meta = jnp.concatenate(
        [
            expert_ids[:, 0].transpose(0, 2, 1).reshape(4, rows).astype(F32),
            gate_weights[:, 0].transpose(0, 2, 1).reshape(4, rows),
            jnp.broadcast_to(lengths.astype(F32)[:, None], (8, rows)),
        ],
        axis=0,
    )
    vmem = pl.BlockSpec(memory_space=pltpu.VMEM)
    anywhere = pl.BlockSpec(memory_space=pl.ANY)
    dma = pltpu.SemaphoreType.DMA
    out = pl.pallas_call(
        kernel,
        out_shape=jax.ShapeDtypeStruct((rows, width), BF16),
        in_specs=[anywhere, vmem, vmem, anywhere, anywhere, anywhere],
        out_specs=anywhere,
        scratch_shapes=[
            pltpu.VMEM((rows, width), BF16),
            pltpu.VMEM((2, 2, rows, half), BF16),
            pltpu.VMEM((3, 2, rows, 128), F32),
            pltpu.VMEM((2, rows, 128), F32),
            pltpu.VMEM((2, 16, rows), F32),
            pltpu.VMEM((2, 16, rows), F32),
            pltpu.VMEM((16, rows), F32),
            pltpu.VMEM((1, width), F32),
            pltpu.VMEM((width, 2 * hid), BF16),
            pltpu.VMEM((2 * hid, half), BF16),
            pltpu.VMEM((2 * rows, half), BF16),
            pltpu.VMEM((CHIPS, block, 2 * rows), BF16),
            pltpu.VMEM((CHIPS, block, 2 * rows), F32),
            pltpu.VMEM((2, 4 * rows, CHIPS * block), BF16),
            pltpu.VMEM((CHIPS, block, half), BF16),
            pltpu.VMEM((2, 2, CHIPS, block, half), BF16),
            pltpu.VMEM((2, CHIPS * block, 2 * hid), BF16),
            pltpu.VMEM((CHUNKS, CHIPS, block, cw), BF16),
            pltpu.VMEM((2, CHUNKS, CHIPS, block, cw), BF16),
            pltpu.VMEM((2, CHUNKS, 2, rows, cw), BF16),
            dma((3,)),
            dma, dma,
            dma, dma,
            dma((3,)), dma((3,)),
            dma((5,)), dma((5,)),
            dma((CHIPS,)), dma((2, CHIPS)),
            dma((CHIPS,)), dma((2, CHIPS)),
            dma((GROUPS,)), dma((2, GROUPS)),
            dma((CHUNKS, CHIPS)), dma((2, CHUNKS, CHIPS)),
            dma((CHUNKS,)), dma((CHUNKS,)),
            dma((CHUNKS, 2)), dma((CHUNKS, 2)),
            dma((3 + CHUNKS,)),
        ],
        compiler_params=pltpu.CompilerParams(
            collective_id=0, has_side_effects=True, vmem_limit_bytes=58 * 2**20
        ),
        cost_estimate=pl.CostEstimate(
            flops=2 * 2 * CHIPS * block * width * 3 * hid, bytes_accessed=3 * width * hid * 2 + 2 * rows * width * 2,
            transcendentals=0,
        ),
    )(state[0], meta, gain, w_gate[0], w_up[0], w_down[0])
    return out[None]


def solution(mesh):
    return jax.shard_map(
        body,
        mesh=mesh,
        in_specs=(
            P("section", "expert", None),
            P("section"),
            P("section", None),
            P("section", None, "expert"),
            P("section", None, "expert"),
            P("section", "expert", None),
            P(None, "section", "expert", None),
            P(None, "section", "expert", None),
        ),
        out_specs=P("section", "expert", None),
        check_vma=False,
    )
```

time: 178 us -> 168 us (0.944)
  the two profiles are of different devices: /device:TPU:57 before, /device:TPU:1 now
where the time goes in v2:
time: 168 us; the launch traced here: 165 us
  Pallas kernels  160 us (95%)
  local copies, waits for them, and re-layouts  2.37 us (1%)
  other arithmetic  2.03 us (1%)
    pallas_call x1, Pallas kernels, body(): pl.pallas_call(kernel, out_shape=jax.ShapeDtypeStruct((rows, width), BF16...  160 us

profile of v2, /device:TPU:1, one launch (start us, length us, event | category | flops | bytes accessed | tf_op | source)
XLA Modules:
  0.0 165.1 jit_solution(2052106846462274953)
XLA Ops:
  0.7 0.1 pad.2.clone
  0.7 0.7 convert_element_type.15
  1.4 1.4 maximum_maximum_fusion.meta_ref
  2.8 160.0 %shard_map.82 = bf16[128,4096]{1,0:T(8,128)(2,1)} custom-call(bf16[128,4096]{1,0:T(8,128)(2,1)} %bitcast.22, f32[16,128]{1,0:T(8,128)} %maximum_maximum_fusion.meta_ref, f32[1,4096]{1,0:T(1,128)} %gain_ref.1, bf16[4096,384]{1,0:T(8,128)(2,1)} %bitcast.19, bf16[4096,384]{1,0:T(8,128)(2,1)} %bitcast.20, bf16[384,4096]{1,0:T(8,128)(2,1)} %bitcast.21), custom_call_target="tpu_custom_call" | custom-call | flops 12079595520 | bytes 11534336 | tf_op jit(solution)/shard_map/pallas_call | solution.py:444
  162.8 2.3 %copy.11 = bf16[1,128,4096]{2,1,0:T(8,128)(2,1)} copy(bf16[1,128,4096]{2,1,0:T(8,128)(2,1)} %bitcast.16) | data formatting | bytes 2097152
  (1 shorter events, 0.0 us)

commit v3 on v2

--- a/solution.py
+++ b/solution.py
@@ -12,6 +12,8 @@
 OWN = 2
 CHUNKS = 8
 GROUPS = 4
+STREAM = 4
+LAG = 1
 EARLY = 2
 MESH = pl.DeviceIdType.MESH
 F32 = jnp.float32
@@ -25,9 +27,9 @@
 
 def kernel(
     x_ref, meta_ref, gain_ref, wg_ref, wu_ref, wd_ref, o_ref,
-    xin, xb, ssb, ssl, meta0, meta1, metaz, gain1, wgu, wdn, normed, pick, pickw, pickt,
+    xb, meta0, meta1, metaz, gain_t, wgu, wdn, pick, pickw, pickt,
     packed, arrived, hidden, outgo, back, stage,
-    w_sem, wd_send, wd_recv, x_send, x_recv, ss_send, ss_recv, m_send, m_recv,
+    w_sem, wd_send, wd_recv, x_send, x_recv, m_send, m_recv,
     d_send, d_recv, f_send, f_recv, h_send, h_recv, c_send, c_recv, r_send, r_recv, o_send, o_recv, l_sem,
 ):
     rows = x_ref.shape[0]
@@ -75,9 +77,7 @@
         pltpu.make_async_copy(wd_ref.at[:, pl.ds(mine, half)], wdn.at[pl.ds(hid_at, hid), :], w_sem.at[2]),
     ]
     own_x = pltpu.make_async_copy(x_ref.at[:, pl.ds(mine, half)], xb.at[0, core], l_sem.at[0])
-    whole_x = pltpu.make_async_copy(x_ref, xin, l_sem.at[1])
     own_meta = pltpu.make_async_copy(meta_ref, meta0.at[core], l_sem.at[2])
-    whole_x.start()
     own_x.start()
     own_meta.start()
 
@@ -103,23 +103,17 @@
             greet(device(dz=dz, to=to))
     for copy in weight_copies:
         copy.start()
-    whole_x.wait()
-    xf = xin[...].astype(F32)
-    ssb[0, core] = jnp.broadcast_to(jnp.sum(xf * xf, axis=-1, keepdims=True), (rows, 128))
     pl.semaphore_wait(barrier, 2 * CHIPS + 5)
 
     x_copy = remote(x_ref.at[:, pl.ds(theirs, half)], xb.at[0, core], x_send, x_recv, partner)
     meta_copies = [
         remote(meta_ref, meta0.at[core], m_send.at[0], m_recv.at[0], partner),
         remote(meta_ref, metaz, m_send.at[1], m_recv.at[1], device(dz=1)),
-        remote(gain_ref, gain1, m_send.at[2], m_recv.at[2], device(flip=1)),
-        remote(meta_ref, meta1.at[core], m_send.at[3], m_recv.at[3 + core], device(flip=1, to=core)),
-        remote(meta_ref, meta1.at[core], m_send.at[4], m_recv.at[3 + core], device(flip=1, to=other)),
+        remote(meta_ref, meta1.at[core], m_send.at[2], m_recv.at[2 + core], device(flip=1, to=core)),
+        remote(meta_ref, meta1.at[core], m_send.at[3], m_recv.at[2 + core], device(flip=1, to=other)),
     ]
-    ss_copy = remote(ssb.at[0, core], ssb.at[0, core], ss_send.at[0], ss_recv.at[0], partner)
     meta_copies[0].start()
     x_copy.start()
-    ss_copy.start()
     for copy in meta_copies[1:]:
         copy.start()
     wd_copy = remote(
@@ -172,12 +166,12 @@
         pickt[step, 0 : 2 * rows] = high
         pickt[step, 2 * rows :] = (turned - high.astype(F32)).astype(BF16)
 
-    def norm(step, part, total):
-        gain = gain1 if step else gain_ref
-        scale = lax.rsqrt(total * (1.0 / width) + 1e-06)
-        normed[pl.ds(pl.multiple_of(part * rows, rows), rows), :] = (
-            xb[step, part].astype(F32) * scale * gain[0:1, pl.ds(mine, half)]
-        ).astype(BF16)
+    def scale_weights(j):
+        at = pl.multiple_of(j * 128, 128)
+        column = jnp.sum(
+            jnp.where(lax.broadcasted_iota(jnp.int32, (128, 128), 1) == j, gain_t[...], 0.0), axis=1, keepdims=True
+        )
+        wgu[pl.ds(at, 128), :] = (wgu[pl.ds(at, 128), :].astype(F32) * column).astype(BF16)
 
     own_meta.wait()
     meta_copies[0].wait()
@@ -188,13 +182,7 @@
 
         if step == 0:
             own_x.wait()
-            norm(0, core, ssb[0, core, :, 0:1])
             x_copy.wait()
-            ss_copy.wait()
-            norm(0, other, ssb[0, other, :, 0:1])
-        else:
-            for part in range(2):
-                norm(1, part, jnp.sum(ssb[1, part] + ssb[2, part], axis=-1, keepdims=True))
 
         def dispatch(k):
             dy, fxh = order(k)
@@ -203,9 +191,10 @@
                 device(flip=flip, dy=dy, fxh=fxh),
             )
 
-        for pair in range(CHIPS // 2):
+        for pair in range(0 if step == 0 else STREAM // 2, CHIPS // 2):
             sent = jnp.dot(
-                pick[2 * pair : 2 * pair + 2].reshape(2 * block, 2 * rows), normed[...], preferred_element_type=F32
+                pick[2 * pair : 2 * pair + 2].reshape(2 * block, 2 * rows), xb[step].reshape(2 * rows, half),
+                preferred_element_type=F32,
             ).astype(BF16).reshape(2, block, half)
             for i in range(2):
                 k = 2 * pair + i
@@ -217,9 +206,14 @@
 
         if step == 0:
             turn(0)
+            gains = [gain_ref[0:1, j * 128 : (j + 1) * 128] for j in range(width // 128)]
+            gain_t[...] = jnp.concatenate(gains + [jnp.zeros((128 - len(gains), 128), F32)], axis=0).T
             for copy in weight_copies:
                 copy.wait()
+            loop(0, width // 128, scale_weights)
             wd_copy.wait()
+        else:
+            all_sent(0)
 
         def forward(k, side):
             place = arrived.at[step, side, k]
@@ -249,6 +243,13 @@
             ]
             product = jnp.dot(both[0], wgu[0:half, :], preferred_element_type=F32)
             product = product + jnp.dot(both[1], wgu[half:width, :], preferred_element_type=F32)
+            sums = jnp.zeros((per * block, 128), F32)
+            for side in range(2):
+                for i in range(half // 128):
+                    piece = both[side][:, i * 128 : (i + 1) * 128].astype(F32)
+                    sums = sums + piece * piece
+            total = jnp.sum(sums, axis=-1, keepdims=True)
+            product = product * lax.rsqrt(total * (1.0 / width) + 1e-06)
             value = (jax.nn.silu(product[:, 0:hid]) * product[:, hid:]).astype(BF16)
             hidden[step, pl.ds(pl.multiple_of(g * per * block, per * block), per * block), pl.ds(hid_at, hid)] = value
             share(g, hid_at).start()
@@ -283,16 +284,24 @@
         loop(EARLY, CHUNKS, lambda q: finish(q, 0, GROUPS))
 
         if step == 0:
-            for copy in meta_copies[1:3]:
-                copy.wait()
-            for copy in meta_copies[3:]:
+            meta_copies[1].wait()
+            for copy in meta_copies[2:]:
                 copy.wait_send()
             for part in range(2):
                 remote(
-                    meta_ref, meta1.at[part], m_send.at[3], m_recv.at[3 + part], device(flip=1, to=part)
+                    meta_ref, meta1.at[part], m_send.at[2], m_recv.at[2 + part], device(flip=1, to=part)
                 ).wait_recv()
             choose(1)
             turn(1)
+
+            def dispatched(k):
+                forward(k, core).wait_send()
+
+                @pl.when(k != OWN)
+                def _():
+                    dispatch(k).wait_send()
+
+            loop(0, CHIPS, dispatched)
 
         def relay(q):
             return remote(
@@ -326,12 +335,6 @@
                     + (value[part * rows : (part + 1) * rows] + value[low : low + rows])
                 ).astype(BF16)
                 stage[step, q, part] = new
-                if step == 0:
-                    square = new.astype(F32) * new.astype(F32)
-                    sums = square[:, 0:128]
-                    for i in range(1, cw // 128):
-                        sums = sums + square[:, i * 128 : (i + 1) * 128]
-                    ssl[part] += sums
 
             if step == 0:
 
@@ -354,49 +357,62 @@
                     hand(q, other, 0).start()
                     keep(q).start()
 
+        def stream(q):
+            @pl.when(x_lo == 1)
+            def _():
+                relay(q).wait_recv()
+
+            columns = pl.ds(pl.multiple_of(q * cw, cw), cw)
+            sent = jnp.dot(
+                pick[0:STREAM].reshape(STREAM * block, 2 * rows), xb[1, :, :, columns].reshape(2 * rows, cw),
+                preferred_element_type=F32,
+            ).astype(BF16).reshape(STREAM, block, cw)
+            for k in range(STREAM):
+                dy, fxh = order(k)
+                packed[k, :, columns] = sent[k]
+                remote(
+                    packed.at[k, :, columns], arrived.at[1, core, k, :, columns], d_send.at[k], d_recv.at[1, k],
+                    device(flip=1, dy=dy, fxh=fxh),
+                ).start()
+
         if step == 0:
-            ssl[...] = jnp.zeros_like(ssl)
-        loop(0, CHUNKS, combine)
-
-        def sent_all(k):
-            forward(k, core).wait_send()
-            if step == 0:
-
-                @pl.when(k != OWN)
-                def _():
+
+            def combine_and_stream(q):
+                @pl.when(q < CHUNKS)
+                def _():
+                    combine(q)
+
+                @pl.when(q >= LAG)
+                def _():
+                    stream(q - LAG)
+
+            loop(0, CHUNKS + LAG, combine_and_stream)
+        else:
+            loop(0, CHUNKS, combine)
+
+
+        def all_sent(done):
+            def sent_all(k):
+                if done == 0:
+
+                    @pl.when(k != OWN)
+                    def _():
+                        loop(0, CHUNKS, lambda q: give(q, k).wait_send())
+                else:
+                    forward(k, core).wait_send()
                     dispatch(k).wait_send()
                     loop(0, CHUNKS, lambda q: give(q, k).wait_send())
-            else:
-                dispatch(k).wait_send()
-                loop(0, CHUNKS, lambda q: give(q, k).wait_send())
-
-        def all_sent():
+
             loop(0, CHIPS, sent_all)
             loop(0, GROUPS, lambda g: share(g, hid_at).wait_send())
 
         if step == 0:
-            def sums(to, dz, number, sender):
-                return remote(ssl, ssb.at[1 + sender], ss_send.at[number], ss_recv.at[1 + sender], device(dz=dz, to=to))
-
-            @pl.when(x_lo == 0)
-            def _():
-                sums(other, 0, 1, core).start()
-                ssb[1 + core] = ssl[...]
-                all_sent()
-                sums(other, 0, 1, core).wait_send()
-                sums(other, 0, 1, other).wait_recv()
 
             @pl.when(x_lo == 1)
             def _():
-                sums(core, 1, 1, core).start()
-                sums(other, 1, 2, core).start()
-                all_sent()
-                loop(0, CHUNKS, lambda q: relay(q).wait())
-                for number, sender in ((1, core), (2, other)):
-                    sums(sender, 1, number, core).wait_send()
-                    sums(sender, 1, number, sender).wait_recv()
+                loop(0, CHUNKS, lambda q: relay(q).wait_send())
         else:
-            all_sent()
+            all_sent(1)
 
             @pl.when(x_lo == 0)
             def _():
@@ -447,17 +463,13 @@
         in_specs=[anywhere, vmem, vmem, anywhere, anywhere, anywhere],
         out_specs=anywhere,
         scratch_shapes=[
-            pltpu.VMEM((rows, width), BF16),
             pltpu.VMEM((2, 2, rows, half), BF16),
-            pltpu.VMEM((3, 2, rows, 128), F32),
-            pltpu.VMEM((2, rows, 128), F32),
             pltpu.VMEM((2, 16, rows), F32),
             pltpu.VMEM((2, 16, rows), F32),
             pltpu.VMEM((16, rows), F32),
-            pltpu.VMEM((1, width), F32),
+            pltpu.VMEM((128, 128), F32),
             pltpu.VMEM((width, 2 * hid), BF16),
             pltpu.VMEM((2 * hid, half), BF16),
-            pltpu.VMEM((2 * rows, half), BF16),
             pltpu.VMEM((CHIPS, block, 2 * rows), BF16),
             pltpu.VMEM((CHIPS, block, 2 * rows), F32),
             pltpu.VMEM((2, 4 * rows, CHIPS * block), BF16),
@@ -470,8 +482,7 @@
             dma((3,)),
             dma, dma,
             dma, dma,
-            dma((3,)), dma((3,)),
-            dma((5,)), dma((5,)),
+            dma((4,)), dma((4,)),
             dma((CHIPS,)), dma((2, CHIPS)),
             dma((CHIPS,)), dma((2, CHIPS)),
             dma((GROUPS,)), dma((2, GROUPS)),

time: 168 us -> 185 us (1.10)
  Pallas kernels: 160 us -> 177 us
    pallas_call x1, Pallas kernels: 160 us -> 177 us  [body(): pl.pallas_call(kernel, out_shape=jax.ShapeDtypeStruct((rows, width), BF16...]
where the time goes in v3:
time: 185 us; the launch traced here: 182 us
  Pallas kernels  177 us (96%)
  local copies, waits for them, and re-layouts  2.37 us (1%)
  other arithmetic  2.03 us (1%)
    pallas_call x1, Pallas kernels, body(): pl.pallas_call(kernel, out_shape=jax.ShapeDtypeStruct((rows, width), BF16...  177 us

profile of v3, /device:TPU:1, one launch (start us, length us, event | category | flops | bytes accessed | tf_op | source)
XLA Modules:
  0.0 181.8 jit_solution(12401742965397143758)
XLA Ops:
  0.7 0.1 pad.2.clone
  0.7 0.7 convert_element_type.15
  1.4 1.4 maximum_maximum_fusion.meta_ref
  2.8 176.7 %shard_map.82 = bf16[128,4096]{1,0:T(8,128)(2,1)} custom-call(bf16[128,4096]{1,0:T(8,128)(2,1)} %bitcast.22, f32[16,128]{1,0:T(8,128)} %maximum_maximum_fusion.meta_ref, f32[1,4096]{1,0:T(1,128)} %gain_ref.1, bf16[4096,384]{1,0:T(8,128)(2,1)} %bitcast.19, bf16[4096,384]{1,0:T(8,128)(2,1)} %bitcast.20, bf16[384,4096]{1,0:T(8,128)(2,1)} %bitcast.21), custom_call_target="tpu_custom_call" | custom-call | flops 12079595520 | bytes 11534336 | tf_op jit(solution)/shard_map/pallas_call | solution.py:460
  179.5 2.3 %copy.11 = bf16[1,128,4096]{2,1,0:T(8,128)(2,1)} copy(bf16[1,128,4096]{2,1,0:T(8,128)(2,1)} %bitcast.16) | data formatting | bytes 2097152
  (1 shorter events, 0.0 us)

commit v4 on v3

--- a/solution.py
+++ b/solution.py
@@ -191,18 +191,26 @@
                 device(flip=flip, dy=dy, fxh=fxh),
             )
 
-        for pair in range(0 if step == 0 else STREAM // 2, CHIPS // 2):
+        def pack(first, q, step=step):
+            columns = pl.ds(pl.multiple_of(q * cw, cw), cw)
             sent = jnp.dot(
-                pick[2 * pair : 2 * pair + 2].reshape(2 * block, 2 * rows), xb[step].reshape(2 * rows, half),
-                preferred_element_type=F32,
-            ).astype(BF16).reshape(2, block, half)
-            for i in range(2):
-                k = 2 * pair + i
+                pick[first : first + STREAM].reshape(STREAM * block, 2 * rows),
+                xb[step, :, :, columns].reshape(2 * rows, cw), preferred_element_type=F32,
+            ).astype(BF16).reshape(STREAM, block, cw)
+            for i in range(STREAM):
+                k = first + i
                 if step == 0 and k == OWN:
-                    arrived[0, core, OWN] = sent[i]
-                else:
-                    packed[k] = sent[i]
-                    dispatch(k).start()
+                    arrived[0, core, OWN, :, columns] = sent[i]
+                    continue
+                dy, fxh = order(k)
+                packed[k, :, columns] = sent[i]
+                remote(
+                    packed.at[k, :, columns], arrived.at[step, core, k, :, columns], d_send.at[k], d_recv.at[step, k],
+                    device(flip=step, dy=dy, fxh=fxh),
+                ).start()
+
+        for first in range(0 if step == 0 else STREAM, CHIPS, STREAM):
+            loop(0, CHUNKS, lambda q: pack(first, q))
 
         if step == 0:
             turn(0)
@@ -362,18 +370,7 @@
             def _():
                 relay(q).wait_recv()
 
-            columns = pl.ds(pl.multiple_of(q * cw, cw), cw)
-            sent = jnp.dot(
-                pick[0:STREAM].reshape(STREAM * block, 2 * rows), xb[1, :, :, columns].reshape(2 * rows, cw),
-                preferred_element_type=F32,
-            ).astype(BF16).reshape(STREAM, block, cw)
-            for k in range(STREAM):
-                dy, fxh = order(k)
-                packed[k, :, columns] = sent[k]
-                remote(
-                    packed.at[k, :, columns], arrived.at[1, core, k, :, columns], d_send.at[k], d_recv.at[1, k],
-                    device(flip=1, dy=dy, fxh=fxh),
-                ).start()
+            pack(0, q, 1)
 
         if step == 0:
 

time: 185 us -> 157 us (0.85); the launches traced: 182 us -> 157 us
  Pallas kernels: 177 us -> 152 us
    pallas_call x1, Pallas kernels: 177 us -> 152 us  [body(): pl.pallas_call(kernel, out_shape=jax.ShapeDtypeStruct((rows, width), BF16...]
where the time goes in v4:
time: 157 us
  Pallas kernels  152 us (97%)
  local copies, waits for them, and re-layouts  2.37 us (2%)
  other arithmetic  2.03 us (1%)
    pallas_call x1, Pallas kernels, body(): pl.pallas_call(kernel, out_shape=jax.ShapeDtypeStruct((rows, width), BF16...  152 us

profile of v4, /device:TPU:1, one launch (start us, length us, event | category | flops | bytes accessed | tf_op | source)
XLA Modules:
  0.0 156.6 jit_solution(2032635942125764568)
XLA Ops:
  0.7 0.1 pad.2.clone
  0.7 0.7 convert_element_type.15
  1.4 1.4 maximum_maximum_fusion.meta_ref
  2.8 151.6 %shard_map.82 = bf16[128,4096]{1,0:T(8,128)(2,1)} custom-call(bf16[128,4096]{1,0:T(8,128)(2,1)} %bitcast.22, f32[16,128]{1,0:T(8,128)} %maximum_maximum_fusion.meta_ref, f32[1,4096]{1,0:T(1,128)} %gain_ref.1, bf16[4096,384]{1,0:T(8,128)(2,1)} %bitcast.19, bf16[4096,384]{1,0:T(8,128)(2,1)} %bitcast.20, bf16[384,4096]{1,0:T(8,128)(2,1)} %bitcast.21), custom_call_target="tpu_custom_call" | custom-call | flops 12079595520 | bytes 11534336 | tf_op jit(solution)/shard_map/pallas_call | solution.py:457
  154.3 2.3 %copy.11 = bf16[1,128,4096]{2,1,0:T(8,128)(2,1)} copy(bf16[1,128,4096]{2,1,0:T(8,128)(2,1)} %bitcast.16) | data formatting | bytes 2097152
  (1 shorter events, 0.0 us)

commit v5 on v4

--- a/solution.py
+++ b/solution.py
@@ -11,7 +11,7 @@
 CHIPS = 8
 OWN = 2
 CHUNKS = 8
-GROUPS = 4
+GROUPS = 2
 STREAM = 4
 LAG = 1
 EARLY = 2

time: 157 us -> 167 us (1.064)
  Pallas kernels: 152 us -> 160 us
    pallas_call x1, Pallas kernels: 152 us -> 160 us  [body(): pl.pallas_call(kernel, out_shape=jax.ShapeDtypeStruct((rows, width), BF16...]
where the time goes in v5:
time: 167 us; the launch traced here: 165 us
  Pallas kernels  160 us (96%)
  local copies, waits for them, and re-layouts  2.37 us (1%)
  other arithmetic  2.03 us (1%)
    pallas_call x1, Pallas kernels, body(): pl.pallas_call(kernel, out_shape=jax.ShapeDtypeStruct((rows, width), BF16...  160 us

profile of v5, /device:TPU:1, one launch (start us, length us, event | category | flops | bytes accessed | tf_op | source)
XLA Modules:
  0.0 165.0 jit_solution(16421476479263246830)
XLA Ops:
  0.7 0.1 pad.2.clone
  0.7 0.7 convert_element_type.15
  1.4 1.4 maximum_maximum_fusion.meta_ref
  2.8 159.9 %shard_map.82 = bf16[128,4096]{1,0:T(8,128)(2,1)} custom-call(bf16[128,4096]{1,0:T(8,128)(2,1)} %bitcast.22, f32[16,128]{1,0:T(8,128)} %maximum_maximum_fusion.meta_ref, f32[1,4096]{1,0:T(1,128)} %gain_ref.1, bf16[4096,384]{1,0:T(8,128)(2,1)} %bitcast.19, bf16[4096,384]{1,0:T(8,128)(2,1)} %bitcast.20, bf16[384,4096]{1,0:T(8,128)(2,1)} %bitcast.21), custom_call_target="tpu_custom_call" | custom-call | flops 12079595520 | bytes 11534336 | tf_op jit(solution)/shard_map/pallas_call | solution.py:457
  162.7 2.3 %copy.11 = bf16[1,128,4096]{2,1,0:T(8,128)(2,1)} copy(bf16[1,128,4096]{2,1,0:T(8,128)(2,1)} %bitcast.16) | data formatting | bytes 2097152
  (1 shorter events, 0.0 us)
